TPU v7x, 32 devices: a whole 2x2x4 slice. The times are simulated.
32 devices in a mesh: wide: 8 (over y, x, core), narrow: 4 (over z).
Axes of the slice: x: 2, y: 2, z: 4, core: 2. Of those that a mesh axis runs over, the one named last changes fastest.
Arguments:
- state: float32 [2, 2097152], P(None, ('wide', 'narrow')), may hold values from -6 to 6
- gates: float32 [6, 2, 256, 256], replicated
- gate_bits: int32 [6, 8], replicated, may hold values from 7 to 15, as said below
- slot_plan: int32 [5], replicated, may hold values from 7 to 15, as said below
Outputs:
- final_state: float32 [2, 2097152], P(None, ('wide', 'narrow'))
Inputs may be any that keep to these rules, and one draw needn't show every extreme that they name: `gate_bits`: each gate's row names 8 different positions. `slot_plan`: the first 2 entries differ from one another, and so do the last 3.
All inputs are finite; a program needn't handle non-finite values.
Results may differ from a plain program's by a relative error of at most 0.0001.
Values sent between devices are 32-bit elements; how exact they have to be, the bound alone decides.
A program may use at most 64 MiB of HBM per device.

v0:
```python
import functools

import jax
import jax.numpy as jnp
from jax import lax
from jax.experimental import pallas as pl
from jax.experimental.pallas import tpu as pltpu
from jax.sharding import PartitionSpec as P

LANE_BITS = 7
LANES = 2**LANE_BITS
HALF = LANES // 2
CHUNKS = 2
MESH = pl.DeviceIdType.MESH
F32 = jnp.float32
BF16 = jnp.bfloat16


def log2(value):
    return value.bit_length() - 1


def one_hot(lane_values, rows):
    columns = lane_values.shape[1]
    row = lax.broadcasted_iota(jnp.int32, (rows, columns), 0)
    return jnp.where(row == lane_values, 1.0, 0.0).astype(BF16)


def split(values):
    high = values.astype(BF16)
    return high, (values - high.astype(F32)).astype(BF16)


def dot(a, b):
    return jnp.dot(a, b, preferred_element_type=F32)


class Layout:
    def __init__(self, free, wanted, row_bits):
        self.free = free
        self.row_bits = row_bits
        seen = jnp.int32(1) << free
        left = jnp.int32(row_bits - 2)
        packed = jnp.int32(0)
        for label in wanted:
            new = 1 - ((seen >> label) & 1)
            packed = packed + ((new * left) << (3 * label))
            left = left - new
            seen = seen | (jnp.int32(1) << label)
        for label in range(row_bits):
            new = 1 - ((seen >> label) & 1)
            packed = packed + ((new * left) << (3 * label))
            left = left - new
        self.packed = packed

    def inner(self, label):
        return (self.packed >> (3 * label)) & 7

    def shift(self, label):
        return jnp.where(label == self.free, self.row_bits - 1, self.inner(label))


def local_move(layout, free_next):
    differs = layout.free != free_next
    weights = [jnp.where(differs, 2, 1), jnp.where(differs, 1, 2)]

    def place(label):
        return jnp.where(label == layout.free, layout.row_bits - 2, layout.inner(label))

    return weights, place


def exchange_move(layout, slots, free_next):
    top = len(slots) + 2
    base = layout.row_bits - top
    slot_places = [layout.shift(slot) - base for slot in slots]
    count = jnp.int32(0)
    low = [jnp.int32(0), jnp.int32(0)]
    sent_places = []
    for index in range(top):
        is_slot = jnp.int32(0)
        value = jnp.int32(0)
        for number, slot_place in enumerate(slot_places):
            hit = (slot_place == index).astype(jnp.int32)
            is_slot = is_slot + hit
            value = value + hit * (2 + number)
        sent_places.append(jnp.where(is_slot == 1, value, count))
        for number in range(2):
            low[number] = low[number] + jnp.where(
                (is_slot == 0) & (count == number), 1 << index, 0
            )
        count = count + 1 - is_slot
    send_weights = low + [jnp.int32(1) << slot_place for slot_place in slot_places]

    def look_up(table, position):
        total = jnp.int32(0)
        for index, entry in enumerate(table):
            total = total + jnp.where(position == index, entry, 0)
        return total

    free_place = look_up(sent_places, layout.shift(free_next) - base)
    load_weights = [
        jnp.where(free_place <= index, 2 << index, 1 << index) for index in range(top - 1)
    ] + [jnp.int32(1) << free_place]
    final = [
        place - jnp.where(place > free_place, 1, 0) for place in sent_places
    ]

    def place(label):
        shift = layout.shift(label)
        return jnp.where(shift < base, shift, base + look_up(final, shift - base))

    return send_weights, load_weights, place


def block_number(index, weights):
    total = jnp.int32(0)
    for bit, weight in enumerate(weights):
        if (index >> bit) & 1:
            total = total + weight
    return total & (2 ** len(weights) - 1)


def load_blocks(ref, weights):
    count, rows, _ = ref.shape
    halves = []
    for half in range(2):
        parts = [
            ref[block_number(half * (count // 2) + index, weights)]
            for index in range(count // 2)
        ]
        halves.append(jnp.concatenate(parts, axis=0))
    return jnp.concatenate(halves, axis=1)


def store_blocks(ref, halves):
    count, rows, lanes = ref.shape
    for half in range(2):
        ref[pl.ds(half * (count // 2), count // 2)] = halves[half].reshape(
            count // 2, rows, lanes
        )


def kernel(
    narrow,
    wide,
    bits_ref,
    plan_ref,
    state_hbm,
    gates_hbm,
    out_ref,
    state_ref,
    gates_ref,
    high_ref,
    low_ref,
    local_ref,
    narrow_out,
    narrow_send,
    narrow_recv_0,
    narrow_recv_1,
    wide_out,
    wide_send,
    wide_recv_0,
    wide_recv_1,
    state_sem,
    gate_sem,
    narrow_send_sem,
    narrow_recv_sem,
    wide_send_sem,
    wide_recv_sem,
):
    gate_count, _, dim, _ = gates_ref.shape
    third = gate_count // 3
    qubits = log2(dim)
    rows = state_ref.shape[0] // 2
    row_bits = log2(rows)
    narrow_bits = log2(narrow)
    wide_bits = log2(wide)
    me = {"narrow": lax.axis_index("narrow"), "wide": lax.axis_index("wide")}
    sizes = {"narrow": narrow, "wide": wide}
    narrow_recv = (narrow_recv_0, narrow_recv_1)
    wide_recv = (wide_recv_0, wide_recv_1)

    state_copy = pltpu.make_async_copy(state_hbm, state_ref, state_sem)
    state_copy.start()
    gate_copies = []
    for k in range(gate_count):
        gate_copies.append(
            pltpu.make_async_copy(gates_hbm.at[k], gates_ref.at[k], gate_sem.at[k])
        )
        gate_copies[-1].start()

    barrier = pltpu.get_barrier_semaphore()
    for axis in ("narrow", "wide"):
        for step in range(1, sizes[axis]):
            peer = lax.rem(me[axis] + step, sizes[axis])
            pl.semaphore_signal(
                barrier, inc=1, device_id={axis: peer}, device_id_type=MESH
            )

    targets = [
        [bits_ref[k * qubits + j] - LANE_BITS for j in range(qubits)]
        for k in range(gate_count)
    ]
    free = [sum(range(row_bits)) - sum(targets[k]) for k in range(gate_count)]
    slots = [plan_ref[b] - LANE_BITS for b in range(narrow_bits + wide_bits)]
    crossing = {
        third - 1: slots[:narrow_bits],
        2 * third - 1: slots[narrow_bits:],
    }
    layouts, loads, sends, places = {}, {}, {}, {}

    def plan(k):
        layouts[k] = Layout(free[k], crossing.get(k, []) + [free[k + 1]], row_bits)
        if k in crossing:
            sends[k], loads[k], places[k + 1] = exchange_move(
                layouts[k], crossing[k], free[k + 1]
            )
        else:
            loads[k], places[k + 1] = local_move(layouts[k], free[k + 1])

    lane = lax.broadcasted_iota(jnp.int32, (1, dim), 1)

    def prepare(k):
        gate_copies[k].wait()
        pieces = [split(gates_ref[k, part]) for part in range(2)]
        if k > 0:
            column = sum(((lane >> places[k](targets[k][j])) & 1) << j for j in range(qubits))
            pick = one_hot(column, dim)
            pieces = [
                [dot(piece, pick).astype(BF16) for piece in both] for both in pieces
            ]
        if k < gate_count - 1:
            row = sum(
                ((lane >> j) & 1) << layouts[k].inner(targets[k][j]) for j in range(qubits)
            )
            pick_row = one_hot(row, dim)
            pieces = [
                [dot(pick_row, piece).astype(BF16) for piece in both] for both in pieces
            ]
        for part in range(2):
            high_ref[k, pl.ds(part * dim, dim)] = pieces[part][0]
            low_ref[k, pl.ds(part * dim, dim)] = pieces[part][1]

    first_half = lax.broadcasted_iota(jnp.int32, (dim, LANES), 1) < HALF

    def apply(k, halves):
        high, low = split(halves)
        total = dot(high_ref[k], high) + dot(high_ref[k], low) + dot(low_ref[k], high)
        results = []
        for half in range(2):
            by_real = total[:dim, half * LANES : (half + 1) * LANES]
            by_imag = pltpu.roll(
                total[dim:, half * LANES : (half + 1) * LANES], HALF, 1
            )
            results.append(by_real + jnp.where(first_half, -by_imag, by_imag))
        return results

    def copy_to(axis, chunk, send_ref, recv_ref, send_sems, recv_sems, peer):
        start = pl.ds(peer * 4, 4)
        return pltpu.make_async_remote_copy(
            src_ref=send_ref.at[chunk, start],
            dst_ref=recv_ref[chunk].at[pl.ds(me[axis] * 4, 4)],
            send_sem=send_sems.at[chunk, peer],
            recv_sem=recv_sems.at[chunk, me[axis]],
            device_id={axis: peer},
            device_id_type=MESH,
        )

    def copy_from(axis, chunk, send_ref, recv_ref, send_sems, recv_sems, peer):
        start = pl.ds(peer * 4, 4)
        return pltpu.make_async_remote_copy(
            src_ref=send_ref.at[chunk, start],
            dst_ref=recv_ref[chunk].at[start],
            send_sem=send_sems.at[chunk, peer],
            recv_sem=recv_sems.at[chunk, peer],
            device_id={axis: peer},
            device_id_type=MESH,
        )

    links = {
        "narrow": (narrow_send, narrow_recv, narrow_send_sem, narrow_recv_sem),
        "wide": (wide_send, wide_recv, wide_send_sem, wide_recv_sem),
    }

    def send(k, axis, chunk, out):
        send_ref, recv_ref = links[axis][:2]
        for index in range(out.shape[0]):
            send_ref[chunk, index] = out[block_number(index, sends[k])]
        for step in range(1, sizes[axis]):
            peer = lax.rem(me[axis] + step, sizes[axis])
            copy_to(axis, chunk, *links[axis], peer).start()
        own = pl.ds(me[axis] * 4, 4)
        recv_ref[chunk][own] = send_ref[chunk, own]

    def receive(axis, chunk):
        for step in range(1, sizes[axis]):
            peer = lax.rem(me[axis] + sizes[axis] - step, sizes[axis])
            copy_from(axis, chunk, *links[axis], peer).wait_recv()

    def section(first, chunk, halves, out):
        for k in range(first, first + third):
            results = apply(k, halves)
            if k < first + third - 1:
                held = local_ref.at[first // third, chunk]
                store_blocks(held, results)
                halves = load_blocks(held, loads[k])
        if out is not None:
            store_blocks(out, results)
        return results

    for k in range(third):
        plan(k)
    source = lax.broadcasted_iota(jnp.int32, (1, rows), 1)
    target = ((source >> free[0]) & 1) << (row_bits - 1)
    for j in range(qubits):
        target = target + (((source >> targets[0][j]) & 1) << j)
    order_in = one_hot(target, rows)
    prepare(0)
    state_copy.wait()
    real, imag = (state_ref[pl.ds(part, rows, stride=2), :] for part in range(2))
    whole_half = lax.broadcasted_iota(jnp.int32, (rows, LANES), 1) < HALF
    packed = [
        jnp.where(whole_half, real, pltpu.roll(imag, HALF, 1)),
        jnp.where(whole_half, pltpu.roll(real, HALF, 1), imag),
    ]
    for k in range(1, third):
        prepare(k)
    for chunk in range(CHUNKS):
        high, low = split(packed[chunk])
        ordered = dot(order_in, high) + dot(order_in, low)
        halves = jnp.concatenate([ordered[:dim], ordered[dim:]], axis=1)
        out = narrow_out.at[chunk]
        section(0, chunk, halves, out)
        if chunk == 0:
            pl.semaphore_wait(barrier, narrow + wide - 2)
        send(third - 1, "narrow", chunk, out)

    for k in range(third, gate_count - 1):
        plan(k)
    for k in range(third, gate_count):
        prepare(k)
    source = lax.broadcasted_iota(jnp.int32, (1, rows), 1)
    target = ((source >> (row_bits - 1)) & 1) << free[gate_count - 1]
    for j in range(qubits):
        target = target + (((source >> j) & 1) << targets[gate_count - 1][j])
    order_out = one_hot(target, rows)

    for chunk in range(CHUNKS):
        receive("narrow", chunk)
        halves = load_blocks(narrow_recv[chunk], loads[third - 1])
        out = wide_out.at[chunk]
        section(third, chunk, halves, out)
        send(2 * third - 1, "wide", chunk, out)

    final = []
    for chunk in range(CHUNKS):
        receive("wide", chunk)
        halves = load_blocks(wide_recv[chunk], loads[2 * third - 1])
        results = section(2 * third, chunk, halves, None)
        high, low = split(jnp.concatenate(results, axis=0))
        final.append(dot(order_out, high) + dot(order_out, low))
    out_ref[pl.ds(0, rows, stride=2), :] = jnp.where(
        whole_half, final[0], pltpu.roll(final[1], HALF, 1)
    )
    out_ref[pl.ds(1, rows, stride=2), :] = jnp.where(
        whole_half, pltpu.roll(final[0], HALF, 1), final[1]
    )

    for axis in ("narrow", "wide"):
        for chunk in range(CHUNKS):
            for step in range(1, sizes[axis]):
                peer = lax.rem(me[axis] + step, sizes[axis])
                copy_to(axis, chunk, *links[axis], peer).wait_send()


def shards(state, gates, gate_bits, slot_plan):
    amount = state.shape[1]
    rows = amount // LANES
    narrow = lax.axis_size("narrow")
    wide = lax.axis_size("wide")
    gate_count, _, dim, _ = gates.shape

    def exchange_buffers(size):
        count = 4 * size
        block = (count, rows // count, LANES)
        return [pltpu.VMEM((CHUNKS, *block), F32)] * 2 + [pltpu.VMEM(block, F32)] * CHUNKS

    def sems(size):
        return [pltpu.SemaphoreType.DMA((CHUNKS, size))] * 2

    mixed = state.reshape(2, rows, LANES).transpose(1, 0, 2).reshape(2 * rows, LANES)
    result = pl.pallas_call(
        functools.partial(kernel, narrow, wide),
        out_shape=jax.ShapeDtypeStruct((2 * rows, LANES), F32),
        in_specs=[
            pl.BlockSpec(memory_space=pltpu.SMEM),
            pl.BlockSpec(memory_space=pltpu.SMEM),
            pl.BlockSpec(memory_space=pl.ANY),
            pl.BlockSpec(memory_space=pl.ANY),
        ],
        out_specs=pl.BlockSpec(memory_space=pltpu.VMEM),
        scratch_shapes=[
            pltpu.VMEM((2 * rows, LANES), F32),
            pltpu.VMEM(gates.shape, F32),
            pltpu.VMEM((gate_count, 2 * dim, dim), BF16),
            pltpu.VMEM((gate_count, 2 * dim, dim), BF16),
            pltpu.VMEM((3, CHUNKS, 4, rows // 4, LANES), F32),
            *exchange_buffers(narrow),
            *exchange_buffers(wide),
            pltpu.SemaphoreType.DMA,
            pltpu.SemaphoreType.DMA((gate_count,)),
            *sems(narrow),
            *sems(wide),
        ],
        compiler_params=pltpu.CompilerParams(
            collective_id=0, has_side_effects=True, vmem_limit_bytes=48 * 2**20
        ),
        name="window",
    )(gate_bits.reshape(-1), slot_plan, mixed, gates)
    return result.reshape(rows, 2, LANES).transpose(1, 0, 2).reshape(2, amount)


def solution(mesh):
    return jax.shard_map(
        shards,
        mesh=mesh,
        in_specs=(P(None, ("wide", "narrow")), P(), P(), P()),
        out_specs=P(None, ("wide", "narrow")),
        check_vma=False,
    )
```

profile of v0, /device:TPU:0, one launch (start us, length us, event | category | flops | bytes accessed | tf_op | source)
XLA Modules:
  0.0 33.6 jit_solution(17346154244189012507)
XLA Ops:
  0.0 0.8 %reshape.15.bits_ref = s32[48]{0:T(128)S(1)} reshape(s32[6,8]{1,0:T(8,128)} %param.6) | data formatting | bytes 384 | tf_op jit(solution)/shard_map/reshape | solution.py:420
  0.8 0.0 copy-start
  0.8 1.9 %copy-done = f32[6,2,256,256]{3,2,1,0:T(8,128)S(1)} copy-done((f32[6,2,256,256]{3,2,1,0:T(8,128)S(1)}, f32[6,2,256,256]{3,2,1,0:T(8,128)}, u32[]{:S(2)}) %copy-start) | copy-done | bytes 3145752
  2.7 0.0 copy-start.1
  2.7 1.0 %copy-done.1 = f32[2,65536]{1,0:T(2,128)S(1)} copy-done((f32[2,65536]{1,0:T(2,128)S(1)}, f32[2,65536]{1,0:T(2,128)}, u32[]{:S(2)}) %copy-start.1) | copy-done | bytes 524312
  3.7 0.0 copy-start.2
  3.7 0.7 %copy-done.2 = s32[5]{0:T(128)S(1)} copy-done((s32[5]{0:T(128)S(1)}, s32[5]{0:T(128)}, u32[]{:S(2)}) %copy-start.2) | copy-done | bytes 44
  4.4 28.5 %window.1 = f32[1024,128]{1,0:T(8,128)S(1)} custom-call(s32[48]{0:T(128)S(1)} %reshape.15.bits_ref, s32[5]{0:T(128)S(1)} %copy-done.2, f32[1024,128]{1,0:T(8,128)S(1)} %bitcast.11, f32[6,2,256,256]{3,2,1,0:T(8,128)S(1)} %copy-done), custom_call_target="tpu_custom_call" | custom-call | tf_op jit(solution)/shard_map/window/pallas_call | solution.py:393
  32.8 0.8 %copy.8 = f32[2,65536]{1,0:T(2,128)} copy(f32[2,65536]{1,0:T(2,128)S(1)} %bitcast.10) | data formatting | bytes 1048576
Async XLA Ops:
  0.8 1.9 %copy-start = (f32[6,2,256,256]{3,2,1,0:T(8,128)S(1)}, f32[6,2,256,256]{3,2,1,0:T(8,128)}, u32[]{:S(2)}) copy-start(f32[6,2,256,256]{3,2,1,0:T(8,128)} %gates_hbm.1) | copy-start | bytes 9437188
  2.7 1.0 %copy-start.1 = (f32[2,65536]{1,0:T(2,128)S(1)}, f32[2,65536]{1,0:T(2,128)}, u32[]{:S(2)}) copy-start(f32[2,65536]{1,0:T(2,128)} %param.4) | copy-start | bytes 1572868
  3.7 0.7 %copy-start.2 = (s32[5]{0:T(128)S(1)}, s32[5]{0:T(128)}, u32[]{:S(2)}) copy-start(s32[5]{0:T(128)} %plan_ref.1) | copy-start | bytes 64
where the time goes:
time: 33.9 us; the launch traced here: 33.6 us
  Pallas kernels  28.5 us (84%)
  local copies, waits for them, and re-layouts  5.15 us (15%)
    pallas_call x1, Pallas kernels, shards(): pl.pallas_call(functools.partial(kernel, narrow, wide), out_shape=jax.Sha...  28.5 us
    unnamed x7, local copies, waits for them, and re-layouts  4.38 us
    reshape x1, local copies, waits for them, and re-layouts, shards(): gate_bits.reshape(-1)  0.76 us

commit v1 on v0

--- a/solution.py
+++ b/solution.py
@@ -18,6 +18,16 @@
 
 def log2(value):
     return value.bit_length() - 1
+
+
+def partner(index, distance):
+    result = index
+    bit = 1
+    while bit <= distance:
+        if distance & bit:
+            result = result + bit - 2 * bit * lax.rem(lax.div(index, bit), 2)
+        bit *= 2
+    return result
 
 
 def one_hot(lane_values, rows):
@@ -192,14 +202,14 @@
 
     barrier = pltpu.get_barrier_semaphore()
     for axis in ("narrow", "wide"):
-        for step in range(1, sizes[axis]):
-            peer = lax.rem(me[axis] + step, sizes[axis])
+        for step in reversed(range(1, sizes[axis])):
+            peer = partner(me[axis], step)
             pl.semaphore_signal(
                 barrier, inc=1, device_id={axis: peer}, device_id_type=MESH
             )
 
     targets = [
-        [bits_ref[k * qubits + j] - LANE_BITS for j in range(qubits)]
+        [bits_ref[k, j] - LANE_BITS for j in range(qubits)]
         for k in range(gate_count)
     ]
     free = [sum(range(row_bits)) - sum(targets[k]) for k in range(gate_count)]
@@ -287,15 +297,15 @@
         send_ref, recv_ref = links[axis][:2]
         for index in range(out.shape[0]):
             send_ref[chunk, index] = out[block_number(index, sends[k])]
-        for step in range(1, sizes[axis]):
-            peer = lax.rem(me[axis] + step, sizes[axis])
+        for step in reversed(range(1, sizes[axis])):
+            peer = partner(me[axis], step)
             copy_to(axis, chunk, *links[axis], peer).start()
         own = pl.ds(me[axis] * 4, 4)
         recv_ref[chunk][own] = send_ref[chunk, own]
 
     def receive(axis, chunk):
-        for step in range(1, sizes[axis]):
-            peer = lax.rem(me[axis] + sizes[axis] - step, sizes[axis])
+        for step in reversed(range(1, sizes[axis])):
+            peer = partner(me[axis], step)
             copy_from(axis, chunk, *links[axis], peer).wait_recv()
 
     def section(first, chunk, halves, out):
@@ -369,8 +379,8 @@
 
     for axis in ("narrow", "wide"):
         for chunk in range(CHUNKS):
-            for step in range(1, sizes[axis]):
-                peer = lax.rem(me[axis] + step, sizes[axis])
+            for step in reversed(range(1, sizes[axis])):
+                peer = partner(me[axis], step)
                 copy_to(axis, chunk, *links[axis], peer).wait_send()
 
 
@@ -396,8 +406,8 @@
         in_specs=[
             pl.BlockSpec(memory_space=pltpu.SMEM),
             pl.BlockSpec(memory_space=pltpu.SMEM),
-            pl.BlockSpec(memory_space=pl.ANY),
-            pl.BlockSpec(memory_space=pl.ANY),
+            pl.BlockSpec(memory_space=pltpu.HBM),
+            pl.BlockSpec(memory_space=pltpu.HBM),
         ],
         out_specs=pl.BlockSpec(memory_space=pltpu.VMEM),
         scratch_shapes=[
@@ -414,10 +424,10 @@
             *sems(wide),
         ],
         compiler_params=pltpu.CompilerParams(
-            collective_id=0, has_side_effects=True, vmem_limit_bytes=48 * 2**20
+            collective_id=0, has_side_effects=True, vmem_limit_bytes=60 * 2**20
         ),
         name="window",
-    )(gate_bits.reshape(-1), slot_plan, mixed, gates)
+    )(gate_bits, slot_plan, mixed, gates)
     return result.reshape(rows, 2, LANES).transpose(1, 0, 2).reshape(2, amount)
 
 

time: 33.9 us -> 34.4 us (1.015)
  Pallas kernels: 28.5 us -> 32.3 us
  local copies, waits for them, and re-layouts: 5.15 us -> 1.87 us
    pallas_call x1, Pallas kernels: 28.5 us -> 32.3 us  [shards(): pl.pallas_call(functools.partial(kernel, narrow, wide), out_shape=jax.Sha...]
    unnamed x7 -> x1, local copies, waits for them, and re-layouts: 4.38 us -> 1.87 us
    reshape x1 -> x0, local copies, waits for them, and re-layouts: 0.76 us -> none  [shards(): gate_bits.reshape(-1)]
where the time goes in v1:
time: 34.4 us; the launch traced here: 34.2 us
  Pallas kernels  32.3 us (94%)
  local copies, waits for them, and re-layouts  1.87 us (5%)
    pallas_call x1, Pallas kernels, shards(): pl.pallas_call(functools.partial(kernel, narrow, wide), out_shape=jax.Sha...  32.3 us
    unnamed x1, local copies, waits for them, and re-layouts  1.87 us

profile of v1, /device:TPU:0, one launch (start us, length us, event | category | flops | bytes accessed | tf_op | source)
XLA Modules:
  0.0 34.2 jit_solution(9214205786589327435)
XLA Ops:
  0.0 32.3 %window.1 = f32[1024,128]{1,0:T(8,128)} custom-call(s32[6,8]{1,0:T(8,128)} %bits_ref.1, s32[5]{0:T(128)} %plan_ref.1, f32[1024,128]{1,0:T(8,128)} %bitcast.11, f32[6,2,256,256]{3,2,1,0:T(8,128)} %gates_hbm.1), custom_call_target="tpu_custom_call" | custom-call | tf_op jit(solution)/shard_map/window/pallas_call | solution.py:403
  32.3 1.9 %copy.8 = f32[2,65536]{1,0:T(2,128)} copy(f32[2,65536]{1,0:T(2,128)} %bitcast.10) | data formatting | bytes 1048576

commit v2 on v1

--- a/solution.py
+++ b/solution.py
@@ -154,11 +154,13 @@
 def kernel(
     narrow,
     wide,
-    bits_ref,
-    plan_ref,
+    bits_hbm,
+    plan_hbm,
     state_hbm,
     gates_hbm,
     out_ref,
+    bits_ref,
+    plan_ref,
     state_ref,
     gates_ref,
     high_ref,
@@ -172,6 +174,7 @@
     wide_send,
     wide_recv_0,
     wide_recv_1,
+    table_sem,
     state_sem,
     gate_sem,
     narrow_send_sem,
@@ -191,14 +194,21 @@
     narrow_recv = (narrow_recv_0, narrow_recv_1)
     wide_recv = (wide_recv_0, wide_recv_1)
 
+    table_copies = [
+        pltpu.make_async_copy(bits_hbm, bits_ref, table_sem.at[0]),
+        pltpu.make_async_copy(plan_hbm, plan_ref, table_sem.at[1]),
+    ]
+    for copy in table_copies:
+        copy.start()
+    gate_copies = [
+        pltpu.make_async_copy(gates_hbm.at[k], gates_ref.at[k], gate_sem.at[k])
+        for k in range(gate_count)
+    ]
+    gate_copies[0].start()
     state_copy = pltpu.make_async_copy(state_hbm, state_ref, state_sem)
     state_copy.start()
-    gate_copies = []
-    for k in range(gate_count):
-        gate_copies.append(
-            pltpu.make_async_copy(gates_hbm.at[k], gates_ref.at[k], gate_sem.at[k])
-        )
-        gate_copies[-1].start()
+    for k in range(1, third):
+        gate_copies[k].start()
 
     barrier = pltpu.get_barrier_semaphore()
     for axis in ("narrow", "wide"):
@@ -208,6 +218,8 @@
                 barrier, inc=1, device_id={axis: peer}, device_id_type=MESH
             )
 
+    for copy in table_copies:
+        copy.wait()
     targets = [
         [bits_ref[k, j] - LANE_BITS for j in range(qubits)]
         for k in range(gate_count)
@@ -336,6 +348,8 @@
     ]
     for k in range(1, third):
         prepare(k)
+    for k in range(third, gate_count):
+        gate_copies[k].start()
     for chunk in range(CHUNKS):
         high, low = split(packed[chunk])
         ordered = dot(order_in, high) + dot(order_in, low)
@@ -404,13 +418,15 @@
         functools.partial(kernel, narrow, wide),
         out_shape=jax.ShapeDtypeStruct((2 * rows, LANES), F32),
         in_specs=[
-            pl.BlockSpec(memory_space=pltpu.SMEM),
-            pl.BlockSpec(memory_space=pltpu.SMEM),
+            pl.BlockSpec(memory_space=pltpu.HBM),
+            pl.BlockSpec(memory_space=pltpu.HBM),
             pl.BlockSpec(memory_space=pltpu.HBM),
             pl.BlockSpec(memory_space=pltpu.HBM),
         ],
         out_specs=pl.BlockSpec(memory_space=pltpu.VMEM),
         scratch_shapes=[
+            pltpu.SMEM(gate_bits.shape, jnp.int32),
+            pltpu.SMEM(slot_plan.shape, jnp.int32),
             pltpu.VMEM((2 * rows, LANES), F32),
             pltpu.VMEM(gates.shape, F32),
             pltpu.VMEM((gate_count, 2 * dim, dim), BF16),
@@ -418,16 +434,20 @@
             pltpu.VMEM((3, CHUNKS, 4, rows // 4, LANES), F32),
             *exchange_buffers(narrow),
             *exchange_buffers(wide),
+            pltpu.SemaphoreType.DMA((2,)),
             pltpu.SemaphoreType.DMA,
             pltpu.SemaphoreType.DMA((gate_count,)),
             *sems(narrow),
             *sems(wide),
         ],
         compiler_params=pltpu.CompilerParams(
-            collective_id=0, has_side_effects=True, vmem_limit_bytes=60 * 2**20
+            collective_id=0, has_side_effects=True, vmem_limit_bytes=32 * 2**20
         ),
         name="window",
-    )(gate_bits, slot_plan, mixed, gates)
+    )(*(
+        pltpu.with_memory_space_constraint(value, pltpu.HBM)
+        for value in (gate_bits, slot_plan, mixed, gates)
+    ))
     return result.reshape(rows, 2, LANES).transpose(1, 0, 2).reshape(2, amount)
 
 

time: 34.4 us -> 31.3 us (0.910)
  Pallas kernels: 32.3 us -> 30.4 us
  local copies, waits for them, and re-layouts: 1.87 us -> 0.8 us
    pallas_call x1, Pallas kernels: 32.3 us -> 30.4 us  [shards(): pl.pallas_call(functools.partial(kernel, narrow, wide), out_shape=jax.Sha...]
    unnamed x1, local copies, waits for them, and re-layouts: 1.87 us -> 0.8 us
where the time goes in v2:
time: 31.3 us; the launch traced here: 31.2 us
  Pallas kernels  30.4 us (97%)
  local copies, waits for them, and re-layouts  0.8 us (3%)
    pallas_call x1, Pallas kernels, shards(): pl.pallas_call(functools.partial(kernel, narrow, wide), out_shape=jax.Sha...  30.4 us
    unnamed x1, local copies, waits for them, and re-layouts  0.8 us

profile of v2, /device:TPU:0, one launch (start us, length us, event | category | flops | bytes accessed | tf_op | source)
XLA Modules:
  0.0 31.2 jit_solution(13766838502309501428)
XLA Ops:
  0.0 30.4 %window.1 = f32[1024,128]{1,0:T(8,128)S(1)} custom-call(s32[6,8]{1,0:T(8,128)} %bits_hbm.1, s32[5]{0:T(128)} %plan_hbm.1, f32[1024,128]{1,0:T(8,128)} %bitcast.11, f32[6,2,256,256]{3,2,1,0:T(8,128)} %gates_hbm.1), custom_call_target="tpu_custom_call" | custom-call | tf_op jit(solution)/shard_map/window/pallas_call | solution.py:417
  30.4 0.8 %copy.8 = f32[2,65536]{1,0:T(2,128)} copy(f32[2,65536]{1,0:T(2,128)S(1)} %bitcast.10) | data formatting | bytes 1048576

commit v3 on v2

--- a/solution.py
+++ b/solution.py
@@ -43,6 +43,12 @@
 
 def dot(a, b):
     return jnp.dot(a, b, preferred_element_type=F32)
+
+
+def reorder(order, values):
+    return dot(
+        jnp.concatenate([order, order], axis=1), jnp.concatenate(split(values), axis=0)
+    )
 
 
 class Layout:
@@ -163,8 +169,7 @@
     plan_ref,
     state_ref,
     gates_ref,
-    high_ref,
-    low_ref,
+    matrix_ref,
     local_ref,
     narrow_out,
     narrow_send,
@@ -245,30 +250,30 @@
 
     def prepare(k):
         gate_copies[k].wait()
-        pieces = [split(gates_ref[k, part]) for part in range(2)]
+        both = split(gates_ref[k].reshape(2 * dim, dim))
+        pieces = jnp.concatenate(both, axis=0)
         if k > 0:
             column = sum(((lane >> places[k](targets[k][j])) & 1) << j for j in range(qubits))
-            pick = one_hot(column, dim)
-            pieces = [
-                [dot(piece, pick).astype(BF16) for piece in both] for both in pieces
-            ]
+            pieces = dot(pieces, one_hot(column, dim)).astype(BF16)
+        side = jnp.concatenate(
+            [pieces[index * dim : (index + 1) * dim] for index in range(4)], axis=1
+        )
         if k < gate_count - 1:
             row = sum(
                 ((lane >> j) & 1) << layouts[k].inner(targets[k][j]) for j in range(qubits)
             )
-            pick_row = one_hot(row, dim)
-            pieces = [
-                [dot(pick_row, piece).astype(BF16) for piece in both] for both in pieces
-            ]
+            side = dot(one_hot(row, dim), side).astype(BF16)
         for part in range(2):
-            high_ref[k, pl.ds(part * dim, dim)] = pieces[part][0]
-            low_ref[k, pl.ds(part * dim, dim)] = pieces[part][1]
+            high = side[:, part * dim : (part + 1) * dim]
+            low = side[:, (2 + part) * dim : (3 + part) * dim]
+            for number, piece in enumerate((high, high, low)):
+                matrix_ref[k, pl.ds(part * dim, dim), pl.ds(number * dim, dim)] = piece
 
     first_half = lax.broadcasted_iota(jnp.int32, (dim, LANES), 1) < HALF
 
     def apply(k, halves):
         high, low = split(halves)
-        total = dot(high_ref[k], high) + dot(high_ref[k], low) + dot(low_ref[k], high)
+        total = dot(matrix_ref[k], jnp.concatenate([high, low, high], axis=0))
         results = []
         for half in range(2):
             by_real = total[:dim, half * LANES : (half + 1) * LANES]
@@ -350,9 +355,9 @@
         prepare(k)
     for k in range(third, gate_count):
         gate_copies[k].start()
+    ordered_both = reorder(order_in, jnp.concatenate(packed, axis=1))
     for chunk in range(CHUNKS):
-        high, low = split(packed[chunk])
-        ordered = dot(order_in, high) + dot(order_in, low)
+        ordered = ordered_both[:, chunk * LANES : (chunk + 1) * LANES]
         halves = jnp.concatenate([ordered[:dim], ordered[dim:]], axis=1)
         out = narrow_out.at[chunk]
         section(0, chunk, halves, out)
@@ -382,8 +387,7 @@
         receive("wide", chunk)
         halves = load_blocks(wide_recv[chunk], loads[2 * third - 1])
         results = section(2 * third, chunk, halves, None)
-        high, low = split(jnp.concatenate(results, axis=0))
-        final.append(dot(order_out, high) + dot(order_out, low))
+        final.append(reorder(order_out, jnp.concatenate(results, axis=0)))
     out_ref[pl.ds(0, rows, stride=2), :] = jnp.where(
         whole_half, final[0], pltpu.roll(final[1], HALF, 1)
     )
@@ -429,8 +433,7 @@
             pltpu.SMEM(slot_plan.shape, jnp.int32),
             pltpu.VMEM((2 * rows, LANES), F32),
             pltpu.VMEM(gates.shape, F32),
-            pltpu.VMEM((gate_count, 2 * dim, dim), BF16),
-            pltpu.VMEM((gate_count, 2 * dim, dim), BF16),
+            pltpu.VMEM((gate_count, 2 * dim, 3 * dim), BF16),
             pltpu.VMEM((3, CHUNKS, 4, rows // 4, LANES), F32),
             *exchange_buffers(narrow),
             *exchange_buffers(wide),

time: 31.3 us -> 30.5 us (0.974)
  Pallas kernels: 30.4 us -> 29.6 us
    pallas_call x1, Pallas kernels: 30.4 us -> 29.6 us  [shards(): pl.pallas_call(functools.partial(kernel, narrow, wide), out_shape=jax.Sha...]
where the time goes in v3:
time: 30.5 us; the launch traced here: 30.4 us
  Pallas kernels  29.6 us (97%)
  local copies, waits for them, and re-layouts  0.8 us (3%)
    pallas_call x1, Pallas kernels, shards(): pl.pallas_call(functools.partial(kernel, narrow, wide), out_shape=jax.Sha...  29.6 us
    unnamed x1, local copies, waits for them, and re-layouts  0.8 us

profile of v3, /device:TPU:0, one launch (start us, length us, event | category | flops | bytes accessed | tf_op | source)
XLA Modules:
  0.0 30.4 jit_solution(13730079206326265552)
XLA Ops:
  0.0 29.6 %window.1 = f32[1024,128]{1,0:T(8,128)S(1)} custom-call(s32[6,8]{1,0:T(8,128)} %bits_hbm.1, s32[5]{0:T(128)} %plan_hbm.1, f32[1024,128]{1,0:T(8,128)} %bitcast.11, f32[6,2,256,256]{3,2,1,0:T(8,128)} %gates_hbm.1), custom_call_target="tpu_custom_call" | custom-call | tf_op jit(solution)/shard_map/window/pallas_call | solution.py:421
  29.6 0.8 %copy.8 = f32[2,65536]{1,0:T(2,128)} copy(f32[2,65536]{1,0:T(2,128)S(1)} %bitcast.10) | data formatting | bytes 1048576

commit v4 on v3

--- a/solution.py
+++ b/solution.py
@@ -310,15 +310,19 @@
         "wide": (wide_send, wide_recv, wide_send_sem, wide_recv_sem),
     }
 
-    def send(k, axis, chunk, out):
+    def pack(k, axis, chunk, out):
         send_ref, recv_ref = links[axis][:2]
         for index in range(out.shape[0]):
             send_ref[chunk, index] = out[block_number(index, sends[k])]
+        own = pl.ds(me[axis] * 4, 4)
+        recv_ref[chunk][own] = send_ref[chunk, own]
+
+    def send(axis, chunk):
         for step in reversed(range(1, sizes[axis])):
             peer = partner(me[axis], step)
+            if chunk > 0:
+                copy_to(axis, chunk - 1, *links[axis], peer).wait_send()
             copy_to(axis, chunk, *links[axis], peer).start()
-        own = pl.ds(me[axis] * 4, 4)
-        recv_ref[chunk][own] = send_ref[chunk, own]
 
     def receive(axis, chunk):
         for step in reversed(range(1, sizes[axis])):
@@ -361,13 +365,18 @@
         halves = jnp.concatenate([ordered[:dim], ordered[dim:]], axis=1)
         out = narrow_out.at[chunk]
         section(0, chunk, halves, out)
+        pack(third - 1, "narrow", chunk, out)
         if chunk == 0:
             pl.semaphore_wait(barrier, narrow + wide - 2)
-        send(third - 1, "narrow", chunk, out)
-
-    for k in range(third, gate_count - 1):
-        plan(k)
-    for k in range(third, gate_count):
+        else:
+            for k in range(third, 2 * third):
+                plan(k)
+                prepare(k)
+        send("narrow", chunk)
+
+    for k in range(2 * third, gate_count):
+        if k < gate_count - 1:
+            plan(k)
         prepare(k)
     source = lax.broadcasted_iota(jnp.int32, (1, rows), 1)
     target = ((source >> (row_bits - 1)) & 1) << free[gate_count - 1]
@@ -380,7 +389,8 @@
         halves = load_blocks(narrow_recv[chunk], loads[third - 1])
         out = wide_out.at[chunk]
         section(third, chunk, halves, out)
-        send(2 * third - 1, "wide", chunk, out)
+        pack(2 * third - 1, "wide", chunk, out)
+        send("wide", chunk)
 
     final = []
     for chunk in range(CHUNKS):
@@ -396,10 +406,9 @@
     )
 
     for axis in ("narrow", "wide"):
-        for chunk in range(CHUNKS):
-            for step in reversed(range(1, sizes[axis])):
-                peer = partner(me[axis], step)
-                copy_to(axis, chunk, *links[axis], peer).wait_send()
+        for step in reversed(range(1, sizes[axis])):
+            peer = partner(me[axis], step)
+            copy_to(axis, CHUNKS - 1, *links[axis], peer).wait_send()
 
 
 def shards(state, gates, gate_bits, slot_plan):

time: 30.5 us -> 30.8 us (level)
  no operation moved by 1% of the time
where the time goes in v4:
time: 30.8 us; the launch traced here: 30.6 us
  Pallas kernels  29.8 us (97%)
  local copies, waits for them, and re-layouts  0.8 us (3%)
    pallas_call x1, Pallas kernels, shards(): pl.pallas_call(functools.partial(kernel, narrow, wide), out_shape=jax.Sha...  29.8 us
    unnamed x1, local copies, waits for them, and re-layouts  0.8 us

profile of v4, /device:TPU:0, one launch (start us, length us, event | category | flops | bytes accessed | tf_op | source)
XLA Modules:
  0.0 30.6 jit_solution(13760357524535767670)
XLA Ops:
  0.0 29.8 %window.1 = f32[1024,128]{1,0:T(8,128)S(1)} custom-call(s32[6,8]{1,0:T(8,128)} %bits_hbm.1, s32[5]{0:T(128)} %plan_hbm.1, f32[1024,128]{1,0:T(8,128)} %bitcast.11, f32[6,2,256,256]{3,2,1,0:T(8,128)} %gates_hbm.1), custom_call_target="tpu_custom_call" | custom-call | tf_op jit(solution)/shard_map/window/pallas_call | solution.py:430
  29.8 0.8 %copy.8 = f32[2,65536]{1,0:T(2,128)} copy(f32[2,65536]{1,0:T(2,128)S(1)} %bitcast.10) | data formatting | bytes 1048576

commit v5 on v3

--- a/solution.py
+++ b/solution.py
@@ -28,6 +28,32 @@
             result = result + bit - 2 * bit * lax.rem(lax.div(index, bit), 2)
         bit *= 2
     return result
+
+
+def line_order(index, size):
+    mirrored = index >= size // 2
+    place = jnp.where(mirrored, size - 1 - index, index)
+    extra = size - 1 - 2 * place
+    order = []
+    for number in range(size - 1):
+        later = jnp.maximum(number - extra, 0)
+        distance = place - lax.div(later, 2)
+        near = jnp.where(lax.rem(later, 2) == 0, place - distance, place + distance)
+        peer = jnp.where(number < extra, size - 1 - number, near)
+        order.append(jnp.where(mirrored, size - 1 - peer, peer))
+    return order
+
+
+def box_order(index, size):
+    upper = log2(size) - 1
+    odd = lax.rem(index, 2) == 1
+    order = []
+    for distance in reversed(range(1, size)):
+        turned = distance & 1
+        for bit in range(upper):
+            turned |= ((distance >> (1 + bit)) & 1) << (upper - bit)
+        order.append(jnp.where(odd, partner(index, turned), partner(index, distance)))
+    return order
 
 
 def one_hot(lane_values, rows):
@@ -195,7 +221,10 @@
     narrow_bits = log2(narrow)
     wide_bits = log2(wide)
     me = {"narrow": lax.axis_index("narrow"), "wide": lax.axis_index("wide")}
-    sizes = {"narrow": narrow, "wide": wide}
+    peers = {
+        "narrow": line_order(me["narrow"], narrow),
+        "wide": box_order(me["wide"], wide),
+    }
     narrow_recv = (narrow_recv_0, narrow_recv_1)
     wide_recv = (wide_recv_0, wide_recv_1)
 
@@ -217,8 +246,7 @@
 
     barrier = pltpu.get_barrier_semaphore()
     for axis in ("narrow", "wide"):
-        for step in reversed(range(1, sizes[axis])):
-            peer = partner(me[axis], step)
+        for peer in peers[axis]:
             pl.semaphore_signal(
                 barrier, inc=1, device_id={axis: peer}, device_id_type=MESH
             )
@@ -314,15 +342,13 @@
         send_ref, recv_ref = links[axis][:2]
         for index in range(out.shape[0]):
             send_ref[chunk, index] = out[block_number(index, sends[k])]
-        for step in reversed(range(1, sizes[axis])):
-            peer = partner(me[axis], step)
+        for peer in peers[axis]:
             copy_to(axis, chunk, *links[axis], peer).start()
         own = pl.ds(me[axis] * 4, 4)
         recv_ref[chunk][own] = send_ref[chunk, own]
 
     def receive(axis, chunk):
-        for step in reversed(range(1, sizes[axis])):
-            peer = partner(me[axis], step)
+        for peer in peers[axis]:
             copy_from(axis, chunk, *links[axis], peer).wait_recv()
 
     def section(first, chunk, halves, out):
@@ -397,8 +423,7 @@
 
     for axis in ("narrow", "wide"):
         for chunk in range(CHUNKS):
-            for step in reversed(range(1, sizes[axis])):
-                peer = partner(me[axis], step)
+            for peer in peers[axis]:
                 copy_to(axis, chunk, *links[axis], peer).wait_send()
 
 

time: 30.5 us -> 28.9 us (0.948)
  Pallas kernels: 29.6 us -> 28 us
    pallas_call x1, Pallas kernels: 29.6 us -> 28 us  [shards(): pl.pallas_call(functools.partial(kernel, narrow, wide), out_shape=jax.Sha...]
where the time goes in v5:
time: 28.9 us; the launch traced here: 28.8 us
  Pallas kernels  28 us (97%)
  local copies, waits for them, and re-layouts  0.8 us (3%)
    pallas_call x1, Pallas kernels, shards(): pl.pallas_call(functools.partial(kernel, narrow, wide), out_shape=jax.Sha...  28 us
    unnamed x1, local copies, waits for them, and re-layouts  0.8 us

profile of v5, /device:TPU:0, one launch (start us, length us, event | category | flops | bytes accessed | tf_op | source)
XLA Modules:
  0.0 28.8 jit_solution(14458352215891009652)
XLA Ops:
  0.0 28.0 %window.1 = f32[1024,128]{1,0:T(8,128)S(1)} custom-call(s32[6,8]{1,0:T(8,128)} %bits_hbm.1, s32[5]{0:T(128)} %plan_hbm.1, f32[1024,128]{1,0:T(8,128)} %bitcast.11, f32[6,2,256,256]{3,2,1,0:T(8,128)} %gates_hbm.1), custom_call_target="tpu_custom_call" | custom-call | tf_op jit(solution)/shard_map/window/pallas_call | solution.py:446
  28.0 0.8 %copy.8 = f32[2,65536]{1,0:T(2,128)} copy(f32[2,65536]{1,0:T(2,128)S(1)} %bitcast.10) | data formatting | bytes 1048576

commit v6 on v5

--- a/solution.py
+++ b/solution.py
@@ -338,14 +338,16 @@
         "wide": (wide_send, wide_recv, wide_send_sem, wide_recv_sem),
     }
 
-    def send(k, axis, chunk, out):
+    def pack(k, axis, chunk, out):
         send_ref, recv_ref = links[axis][:2]
         for index in range(out.shape[0]):
             send_ref[chunk, index] = out[block_number(index, sends[k])]
-        for peer in peers[axis]:
-            copy_to(axis, chunk, *links[axis], peer).start()
         own = pl.ds(me[axis] * 4, 4)
         recv_ref[chunk][own] = send_ref[chunk, own]
+
+    def send(axis, chunk, some):
+        for peer in some:
+            copy_to(axis, chunk, *links[axis], peer).start()
 
     def receive(axis, chunk):
         for peer in peers[axis]:
@@ -361,6 +363,10 @@
         if out is not None:
             store_blocks(out, results)
         return results
+
+    late = lax.rem(me["wide"], 2) == 1
+    cut = (narrow - 1 + 2) // 3
+    first_peers, other_peers = peers["narrow"][:cut], peers["narrow"][cut:]
 
     for k in range(third):
         plan(k)
@@ -389,7 +395,14 @@
         section(0, chunk, halves, out)
         if chunk == 0:
             pl.semaphore_wait(barrier, narrow + wide - 2)
-        send(third - 1, "narrow", chunk, out)
+        pack(third - 1, "narrow", chunk, out)
+        if chunk == 0:
+            send("narrow", chunk, peers["narrow"])
+        else:
+            send("narrow", chunk, first_peers)
+            pl.when(jnp.logical_not(late))(
+                functools.partial(send, "narrow", chunk, other_peers)
+            )
 
     for k in range(third, gate_count - 1):
         plan(k)
@@ -406,7 +419,10 @@
         halves = load_blocks(narrow_recv[chunk], loads[third - 1])
         out = wide_out.at[chunk]
         section(third, chunk, halves, out)
-        send(2 * third - 1, "wide", chunk, out)
+        pack(2 * third - 1, "wide", chunk, out)
+        send("wide", chunk, peers["wide"])
+        if chunk == 0:
+            pl.when(late)(functools.partial(send, "narrow", CHUNKS - 1, other_peers))
 
     final = []
     for chunk in range(CHUNKS):

time: 28.9 us -> 27.8 us (0.962)
  Pallas kernels: 28 us -> 26.8 us
    pallas_call x1, Pallas kernels: 28 us -> 26.8 us  [shards(): pl.pallas_call(functools.partial(kernel, narrow, wide), out_shape=jax.Sha...]
where the time goes in v6:
time: 27.8 us; the launch traced here: 27.6 us
  Pallas kernels  26.8 us (96%)
  local copies, waits for them, and re-layouts  0.8 us (3%)
    pallas_call x1, Pallas kernels, shards(): pl.pallas_call(functools.partial(kernel, narrow, wide), out_shape=jax.Sha...  26.8 us
    unnamed x1, local copies, waits for them, and re-layouts  0.8 us

profile of v6, /device:TPU:0, one launch (start us, length us, event | category | flops | bytes accessed | tf_op | source)
XLA Modules:
  0.0 27.6 jit_solution(10521733549002528247)
XLA Ops:
  0.0 26.8 %window.1 = f32[1024,128]{1,0:T(8,128)S(1)} custom-call(s32[6,8]{1,0:T(8,128)} %bits_hbm.1, s32[5]{0:T(128)} %plan_hbm.1, f32[1024,128]{1,0:T(8,128)} %bitcast.11, f32[6,2,256,256]{3,2,1,0:T(8,128)} %gates_hbm.1), custom_call_target="tpu_custom_call" | custom-call | tf_op jit(solution)/shard_map/window/pallas_call | solution.py:462
  26.8 0.8 %copy.8 = f32[2,65536]{1,0:T(2,128)} copy(f32[2,65536]{1,0:T(2,128)S(1)} %bitcast.10) | data formatting | bytes 1048576

commit v7 on v6

--- a/solution.py
+++ b/solution.py
@@ -30,7 +30,7 @@
     return result
 
 
-def line_order(index, size):
+def line_order(index, size, inner):
     mirrored = index >= size // 2
     place = jnp.where(mirrored, size - 1 - index, index)
     extra = size - 1 - 2 * place
@@ -38,7 +38,7 @@
     for number in range(size - 1):
         later = jnp.maximum(number - extra, 0)
         distance = place - lax.div(later, 2)
-        near = jnp.where(lax.rem(later, 2) == 0, place - distance, place + distance)
+        near = jnp.where(lax.rem(later, 2) == inner, place - distance, place + distance)
         peer = jnp.where(number < extra, size - 1 - number, near)
         order.append(jnp.where(mirrored, size - 1 - peer, peer))
     return order
@@ -222,7 +222,7 @@
     wide_bits = log2(wide)
     me = {"narrow": lax.axis_index("narrow"), "wide": lax.axis_index("wide")}
     peers = {
-        "narrow": line_order(me["narrow"], narrow),
+        "narrow": line_order(me["narrow"], narrow, lax.rem(me["wide"], 2)),
         "wide": box_order(me["wide"], wide),
     }
     narrow_recv = (narrow_recv_0, narrow_recv_1)

time: 27.8 us -> 27.8 us (level)
  no operation moved by 1% of the time
where the time goes in v7:
time: 27.8 us; the launch traced here: 27.6 us
  Pallas kernels  26.8 us (96%)
  local copies, waits for them, and re-layouts  0.8 us (3%)
    pallas_call x1, Pallas kernels, shards(): pl.pallas_call(functools.partial(kernel, narrow, wide), out_shape=jax.Sha...  26.8 us
    unnamed x1, local copies, waits for them, and re-layouts  0.8 us

profile of v7, /device:TPU:0, one launch (start us, length us, event | category | flops | bytes accessed | tf_op | source)
XLA Modules:
  0.0 27.6 jit_solution(12748338394977154343)
XLA Ops:
  0.0 26.8 %window.1 = f32[1024,128]{1,0:T(8,128)S(1)} custom-call(s32[6,8]{1,0:T(8,128)} %bits_hbm.1, s32[5]{0:T(128)} %plan_hbm.1, f32[1024,128]{1,0:T(8,128)} %bitcast.11, f32[6,2,256,256]{3,2,1,0:T(8,128)} %gates_hbm.1), custom_call_target="tpu_custom_call" | custom-call | tf_op jit(solution)/shard_map/window/pallas_call | solution.py:462
  26.8 0.8 %copy.8 = f32[2,65536]{1,0:T(2,128)} copy(f32[2,65536]{1,0:T(2,128)S(1)} %bitcast.10) | data formatting | bytes 1048576

commit v8 on v7

--- a/solution.py
+++ b/solution.py
@@ -339,9 +339,12 @@
     }
 
     def pack(k, axis, chunk, out):
-        send_ref, recv_ref = links[axis][:2]
+        send_ref = links[axis][0]
         for index in range(out.shape[0]):
             send_ref[chunk, index] = out[block_number(index, sends[k])]
+
+    def keep(axis, chunk):
+        send_ref, recv_ref = links[axis][:2]
         own = pl.ds(me[axis] * 4, 4)
         recv_ref[chunk][own] = send_ref[chunk, own]
 
@@ -350,6 +353,7 @@
             copy_to(axis, chunk, *links[axis], peer).start()
 
     def receive(axis, chunk):
+        keep(axis, chunk)
         for peer in peers[axis]:
             copy_from(axis, chunk, *links[axis], peer).wait_recv()
 
@@ -429,7 +433,9 @@
         receive("wide", chunk)
         halves = load_blocks(wide_recv[chunk], loads[2 * third - 1])
         results = section(2 * third, chunk, halves, None)
-        final.append(reorder(order_out, jnp.concatenate(results, axis=0)))
+        pieces = jnp.concatenate(split(jnp.concatenate(results, axis=0)), axis=1)
+        ordered = dot(order_out, pieces)
+        final.append(ordered[:, :LANES] + ordered[:, LANES:])
     out_ref[pl.ds(0, rows, stride=2), :] = jnp.where(
         whole_half, final[0], pltpu.roll(final[1], HALF, 1)
     )

time: 27.8 us -> 27.5 us (0.989)
  no operation moved by 1% of the time
where the time goes in v8:
time: 27.5 us; the launch traced here: 27.4 us
  Pallas kernels  26.6 us (97%)
  local copies, waits for them, and re-layouts  0.8 us (3%)
    pallas_call x1, Pallas kernels, shards(): pl.pallas_call(functools.partial(kernel, narrow, wide), out_shape=jax.Sha...  26.6 us
    unnamed x1, local copies, waits for them, and re-layouts  0.8 us

profile of v8, /device:TPU:0, one launch (start us, length us, event | category | flops | bytes accessed | tf_op | source)
XLA Modules:
  0.0 27.4 jit_solution(10241550532957700160)
XLA Ops:
  0.0 26.6 %window.1 = f32[1024,128]{1,0:T(8,128)S(1)} custom-call(s32[6,8]{1,0:T(8,128)} %bits_hbm.1, s32[5]{0:T(128)} %plan_hbm.1, f32[1024,128]{1,0:T(8,128)} %bitcast.11, f32[6,2,256,256]{3,2,1,0:T(8,128)} %gates_hbm.1), custom_call_target="tpu_custom_call" | custom-call | tf_op jit(solution)/shard_map/window/pallas_call | solution.py:468
  26.6 0.8 %copy.8 = f32[2,65536]{1,0:T(2,128)} copy(f32[2,65536]{1,0:T(2,128)S(1)} %bitcast.10) | data formatting | bytes 1048576

commit v9 on v8

--- a/solution.py
+++ b/solution.py
@@ -370,7 +370,8 @@
 
     late = lax.rem(me["wide"], 2) == 1
     cut = (narrow - 1 + 2) // 3
-    first_peers, other_peers = peers["narrow"][:cut], peers["narrow"][cut:]
+    first_peers, other_peers = peers["narrow"][:cut], peers["narrow"][cut : 2 * cut]
+    last_peers = peers["narrow"][2 * cut :]
 
     for k in range(third):
         plan(k)
@@ -427,6 +428,7 @@
         send("wide", chunk, peers["wide"])
         if chunk == 0:
             pl.when(late)(functools.partial(send, "narrow", CHUNKS - 1, other_peers))
+            send("narrow", CHUNKS - 1, last_peers)
 
     final = []
     for chunk in range(CHUNKS):

time: 27.5 us -> 27.7 us (level)
  no operation moved by 1% of the time
where the time goes in v9:
time: 27.7 us; the launch traced here: 27.4 us
  Pallas kernels  26.6 us (96%)
  local copies, waits for them, and re-layouts  0.8 us (3%)
    pallas_call x1, Pallas kernels, shards(): pl.pallas_call(functools.partial(kernel, narrow, wide), out_shape=jax.Sha...  26.6 us
    unnamed x1, local copies, waits for them, and re-layouts  0.8 us

profile of v9, /device:TPU:0, one launch (start us, length us, event | category | flops | bytes accessed | tf_op | source)
XLA Modules:
  0.0 27.4 jit_solution(1012815318959273777)
XLA Ops:
  0.0 26.6 %window.1 = f32[1024,128]{1,0:T(8,128)S(1)} custom-call(s32[6,8]{1,0:T(8,128)} %bits_hbm.1, s32[5]{0:T(128)} %plan_hbm.1, f32[1024,128]{1,0:T(8,128)} %bitcast.11, f32[6,2,256,256]{3,2,1,0:T(8,128)} %gates_hbm.1), custom_call_target="tpu_custom_call" | custom-call | tf_op jit(solution)/shard_map/window/pallas_call | solution.py:470
  26.6 0.8 %copy.8 = f32[2,65536]{1,0:T(2,128)} copy(f32[2,65536]{1,0:T(2,128)S(1)} %bitcast.10) | data formatting | bytes 1048576
